TPU v7x, 512 devices: a whole 4x8x8 slice. The times are simulated.
512 devices in a mesh: gx: 32 (over z, x), gy: 16 (over y, core).
Axes of the slice: x: 4, y: 8, z: 8, core: 2. Of those that a mesh axis runs over, the one named last changes fastest.
Arguments:
- fields: bfloat16 [4, 256, 512, 256], P(None, 'gx', 'gy'), may hold values from -6 to 6
- rows_live: int32 [32], replicated, may hold values from 4 to 8, as said below
- cols_live: int32 [16], replicated, may hold values from 16 to 32, as said below
- weight: bfloat16 [32, 108], replicated, may hold values from -0.625 to 0.625
- bias: float32 [32], replicated, may hold values from -3 to 3
- grad_out: bfloat16 [32, 128, 256, 128], P('gy', 'gx'), may hold values from -0.0234375 to 0.0234375
Outputs:
- stem: bfloat16 [32, 128, 256, 128], P('gy', 'gx')
- weight_grad: float32 [32, 108], P('gy')
- bias_grad: float32 [32], P('gy')
Inputs may be any that keep to these rules, and one draw needn't show every extreme that they name: `rows_live`: every entry is even, and some entry equals 8. `cols_live`: every entry is even, and some entry equals 32.
All inputs are finite; a program needn't handle non-finite values.
Results may differ from a plain program's by a relative error of at most 0.0054.
Values may be sent and summed in bfloat16 or wider, within the bound.
A program may use at most 64 MiB of HBM per device.

v0:
```python
import jax
import jax.numpy as jnp
from jax import lax
from jax.sharding import PartitionSpec as P


def from_behind(block, axis, distance):
    devices = range(lax.axis_size(axis))
    route = [(i - distance, i) for i in devices if i - distance in devices]
    return lax.ppermute(block, axis, route)


def extend(data, border, count, dim):
    length = data.shape[dim]
    border_wide = jnp.expand_dims(border, dim)
    joined = jnp.concatenate([jnp.zeros_like(border_wide), data], axis=dim)
    shape = [1] * joined.ndim
    shape[dim] = length + 1
    places = jnp.arange(length + 1, dtype=jnp.int32).reshape(shape)
    edge_at = length - count
    kept = jnp.where(places > edge_at, joined, jnp.zeros_like(joined))
    return jnp.where(places == edge_at, border_wide, kept)


def taps(padded, axes, halves):
    pieces = []
    for off_x in range(3):
        for off_y in range(3):
            for off_z in range(3):
                piece = padded
                for axis_no, offset, half in zip(axes, (off_x, off_y, off_z), halves):
                    piece = lax.slice_in_dim(piece, offset, offset + 2 * half - 1, 2, axis_no)
                pieces.append(piece)
    return pieces


def local(fields, rows_live, cols_live, weight, bias, grad_out):
    in_chans, cap_x, cap_y, depth = fields.shape
    half_x = cap_x // 2
    half_y = cap_y // 2
    half_z = depth // 2
    out_chans = weight.shape[0]
    tiles_y = lax.axis_size("gy")
    row_count = rows_live[lax.axis_index("gx")]
    above = from_behind(fields[:, cap_x - 1], "gx", 1)
    ext_rows = extend(fields, above, row_count, 1)
    row_ok = jnp.arange(half_x, dtype=jnp.int32) >= half_x - row_count // 2
    col_count = cols_live[lax.axis_index("gy")]
    beside = from_behind(ext_rows[:, :, cap_y - 1], "gy", 1)
    ext_full = extend(ext_rows, beside, col_count, 2)
    padded = jnp.pad(ext_full, ((0, 0), (0, 0), (0, 0), (1, 0)))
    patches = jnp.stack(taps(padded, (1, 2, 3), (half_x, half_y, half_z)), axis=1).reshape(
        in_chans * 27, -1
    )
    conv = jnp.dot(weight, patches, preferred_element_type=jnp.float32) + bias[:, None]
    col_ok = jnp.arange(half_y, dtype=jnp.int32) >= half_y - col_count // 2
    live = (row_ok[:, None] & col_ok[None, :]).reshape(1, half_x, half_y, 1)
    conv = conv.reshape(out_chans, half_x, half_y, half_z)
    pre_local = jnp.where(live, conv, 0.0).astype(jnp.bfloat16)
    regrouped = lax.all_to_all(pre_local, "gy", split_axis=0, concat_axis=2, tiled=True)
    pre_wide = regrouped.astype(jnp.float32)
    sigma = jax.nn.sigmoid(pre_wide)
    stem = (pre_wide * sigma).astype(jnp.bfloat16)
    wide_cols = jnp.arange(half_y, dtype=jnp.int32)[None, :] >= half_y - (cols_live // 2)[:, None]
    wide_live = row_ok.reshape(1, half_x, 1, 1) & wide_cols.reshape(1, 1, tiles_y * half_y, 1)
    slope = sigma * (1.0 + pre_wide * (1.0 - sigma))
    grad_pre = jnp.where(wide_live, grad_out.astype(jnp.float32) * slope, 0.0).astype(jnp.bfloat16)
    returned = lax.all_to_all(grad_pre, "gy", split_axis=2, concat_axis=0, tiled=True)
    flat = returned.reshape(out_chans, -1)
    weight_full = lax.dot_general(
        flat, patches, (((1,), (1,)), ((), ())), preferred_element_type=jnp.float32
    )
    bias_full = jnp.sum(flat.astype(jnp.float32), axis=1)
    weight_part, bias_part = (
        lax.psum_scatter(weight_full, "gy", scatter_dimension=0, tiled=True),
        lax.psum_scatter(bias_full, "gy", scatter_dimension=0, tiled=True),
    )
    weight_grad, bias_grad = lax.psum((weight_part, bias_part), "gx")
    return (stem, weight_grad, bias_grad)


def solution(mesh):
    in_specs = (P(None, "gx", "gy", None), P(), P(), P(), P(), P("gy", "gx", None, None))
    out_specs = (P("gy", "gx", None, None), P("gy", None), P("gy"))
    return jax.shard_map(local, mesh=mesh, in_specs=in_specs, out_specs=out_specs, check_vma=False)
```

profile of v0, /device:TPU:2, one launch (start us, length us, event | category | flops | bytes accessed | tf_op | source)
XLA Modules:
  0.0 272.5 jit_solution(16482650276213598681)
XLA Ops:
  1.5 3.4 %collective-permute-start = (bf16[4,32,256]{2,1,0:T(8,128)(2,1)S(1)}, bf16[4,32,256]{2,1,0:T(8,128)(2,1)S(1)}, u32[]{:S(2)}, u32[]{:S(2)}) collective-permute-start(bf16[4,32,256]{2,1,0:T(8,128)(2,1)S(1)} %slice_bitcast_fusion), channel_id=1, source_target_pairs={{0,16},{16,32},{32,48},{48,64},{64,80},{80,96},{96,112},{112,128},... | collective-permute-start | bytes 196616 | tf_op jit(solution)/shard_map/ppermute | solution.py:10
  19.0 2.5 slice.205
  21.5 2.5 slice.204
  24.1 2.5 slice.203
  27.2 2.5 slice.197
  29.8 2.5 slice.196
  32.3 2.5 slice.195
  34.9 2.5 slice.201
  39.9 2.5 slice.199
  42.8 2.5 slice.192
  45.4 2.5 slice.191
  47.9 2.5 slice.190
  51.1 2.5 slice.184
  56.2 2.5 slice.182
  58.7 2.5 slice.188
  63.8 2.5 slice.186
  66.7 2.5 slice.179
  69.3 2.5 slice.178
  71.8 2.5 slice.177
  75.0 2.7 %slice.171 = bf16[4,4,16,128]{3,2,1,0:T(8,128)(2,1)S(1)} slice(bf16[4,4,16,257]{3,2,1,0:T(8,128)(2,1)S(1)} %slice.168), slice={[0:4:1], [0:4:1], [0:16:1], [2:257:2]} | slice | bytes 131072 | tf_op jit(solution)/shard_map/slice | solution.py:32
  77.7 2.5 slice.170
  80.2 2.5 slice.169
  82.8 2.5 slice.175
  85.3 2.5 slice.174
  87.9 2.5 slice.173
  92.5 2.7 reshape.144
  96.8 11.2 %all-to-all-start = ((bf16[32,4,16,128]{3,2,1,0:T(8,128)(2,1)}), bf16[32,4,16,128]{3,2,1,0:T(8,128)(2,1)S(1)}, u32[]{:S(2)}, u32[]{:S(2)}) async-start(bf16[32,4,16,128]{3,2,1,0:T(8,128)(2,1)} %select_convert_fusion), calls=%async_computation | async-start | bytes 1048576 | tf_op jit(solution)/shard_map/all_to_all | solution.py:60
  108.3 15.7 %all-to-all-done = bf16[32,4,16,128]{3,2,1,0:T(8,128)(2,1)S(1)} async-done(((bf16[32,4,16,128]{3,2,1,0:T(8,128)(2,1)}), bf16[32,4,16,128]{3,2,1,0:T(8,128)(2,1)S(1)}, u32[]{:S(2)}, u32[]{:S(2)}) %all-to-all-start) | async-done | bytes 524320 | tf_op jit(solution)/shard_map/all_to_all | solution.py:60
  126.5 4.2 %all-to-all-start.1 = ((bf16[2,4,256,128]{3,1,0,2:T(4,128)(2,1)}), bf16[2,4,256,128]{3,1,0,2:T(4,128)(2,1)S(1)}, u32[]{:S(2)}, u32[]{:S(2)}) async-start(bf16[2,4,256,128]{3,1,0,2:T(4,128)(2,1)} %get-tuple-element.10), calls=%async_computation.1 | async-start | bytes 1048576 | tf_op jit(solution)/shard_map/all_to_all | solution.py:68
  133.5 13.4 %all-to-all-done.1 = bf16[2,4,256,128]{3,1,0,2:T(4,128)(2,1)S(1)} async-done(((bf16[2,4,256,128]{3,1,0,2:T(4,128)(2,1)}), bf16[2,4,256,128]{3,1,0,2:T(4,128)(2,1)S(1)}, u32[]{:S(2)}, u32[]{:S(2)}) %all-to-all-start.1) | async-done | bytes 524320 | tf_op jit(solution)/shard_map/all_to_all | solution.py:68
  148.2 47.1 %all-reduce.6 = (f32[32,108]{1,0:T(8,128)S(1)}, f32[32]{0:T(128)S(1)}) all-reduce(f32[32,108]{1,0:T(8,128)S(1)} %fusion.11, f32[32]{0:T(128)S(1)} %reduce_sum.12), channel_id=2, replica_groups=mesh['gx'=32,'gy'=16] {'gy'}, use_global_device_ids=true, to_apply=%region_0.1.clone | all-reduce | flops 3488 | bytes 27904
  195.4 77.1 %all-reduce.5 = (f32[2,108]{1,0:T(2,128)}, f32[2]{0:T(128)}) all-reduce(f32[2,108]{1,0:T(2,128)S(1)} %constant_dynamic-slice_fusion, f32[2]{0:T(128)S(1)} %dynamic-slice.3), channel_id=1, replica_groups=mesh['gx'=32,'gy'=16] {'gx'}, use_global_device_ids=true, to_apply=%region_1.2 | all-reduce | flops 218 | bytes 1744 | tf_op jit(solution)/shard_map/psum | solution.py:78
  (83 shorter events, 28.2 us)
Async XLA Ops:
  0.6 94.6 %copy-start = (bf16[32,108]{1,0:T(8,128)(2,1)S(1)}, bf16[32,108]{1,0:T(8,128)(2,1)}, u32[]{:S(2)}) copy-start(bf16[32,108]{1,0:T(8,128)(2,1)} %param.9) | copy-start | bytes 20740
  1.5 12.5 %collective-permute-start = (bf16[4,32,256]{2,1,0:T(8,128)(2,1)S(1)}, bf16[4,32,256]{2,1,0:T(8,128)(2,1)S(1)}, u32[]{:S(2)}, u32[]{:S(2)}) collective-permute-start(bf16[4,32,256]{2,1,0:T(8,128)(2,1)S(1)} %slice_bitcast_fusion), channel_id=1, source_target_pairs={{0,16},{16,32},{32,48},{48,64},{64,80},{80,96},{96,112},{112,128},... | collective-permute-start | bytes 196616 | tf_op jit(solution)/shard_map/ppermute | solution.py:10
  15.3 2.3 collective-permute-start.1
  92.5 2.7 %copy-start.2 = (f32[32]{0:T(128)S(1)}, f32[32]{0:T(128)}, u32[]{:S(2)}) copy-start(f32[32]{0:T(128)} %param.10) | copy-start | bytes 388
  95.6 12.4 %copy-start.3 = (s32[16]{0:T(128)S(1)}, s32[16]{0:T(128)}, u32[]{:S(2)}) copy-start(s32[16]{0:T(128)} %param.8) | copy-start | bytes 196
  95.8 28.5 %copy-start.1 = (bf16[2,4,256,128]{3,2,1,0:T(8,128)(2,1)S(1)}, bf16[2,4,256,128]{3,2,1,0:T(8,128)(2,1)}, u32[]{:S(2)}) copy-start(bf16[2,4,256,128]{3,2,1,0:T(8,128)(2,1)} %param.11) | copy-start | bytes 1572868
  96.8 27.2 %all-to-all-start = ((bf16[32,4,16,128]{3,2,1,0:T(8,128)(2,1)}), bf16[32,4,16,128]{3,2,1,0:T(8,128)(2,1)S(1)}, u32[]{:S(2)}, u32[]{:S(2)}) async-start(bf16[32,4,16,128]{3,2,1,0:T(8,128)(2,1)} %select_convert_fusion), calls=%async_computation | async-start | bytes 1048576 | tf_op jit(solution)/shard_map/all_to_all | solution.py:60
  126.5 20.4 %all-to-all-start.1 = ((bf16[2,4,256,128]{3,1,0,2:T(4,128)(2,1)}), bf16[2,4,256,128]{3,1,0,2:T(4,128)(2,1)S(1)}, u32[]{:S(2)}, u32[]{:S(2)}) async-start(bf16[2,4,256,128]{3,1,0,2:T(4,128)(2,1)} %get-tuple-element.10), calls=%async_computation.1 | async-start | bytes 1048576 | tf_op jit(solution)/shard_map/all_to_all | solution.py:68
where the time goes:
time: 273 us; the launch traced here: 272 us
  blocking collectives  124 us (45%)
  local copies, waits for them, and re-layouts  83.2 us (30%)
  waiting for transfers between devices  29.9 us (11%)
  starting transfers between devices  20.2 us (7%)
  between operations  8.45 us (3%)
  other arithmetic  5.38 us (2%)
    psum x1, blocking collectives, local(): weight_grad, bias_grad = lax.psum((weight_part, bias_part), 'gx')  77.1 us
    slice x37, local copies, waits for them, and re-layouts, taps(): piece = lax.slice_in_dim(piece, offset, offset + 2 * half - 1, 2, axis_no)  72.1 us
    unnamed x1, blocking collectives  47.1 us
    all_to_all x1, waiting for transfers between devices, local(): lax.all_to_all(pre_local, 'gy', split_axis=0, concat_axis=2, tiled=True)  15.7 us
    all_to_all x1, waiting for transfers between devices, local(): lax.all_to_all(grad_pre, 'gy', split_axis=2, concat_axis=0, tiled=True)  13.4 us
    all_to_all x1, starting transfers between devices, local(): lax.all_to_all(pre_local, 'gy', split_axis=0, concat_axis=2, tiled=True)  11.2 us
  transfers between devices with their start and end apart: 4, of which 3 were waited for; matrix products, arithmetic and copies ran while one was open for 2% of the time, Pallas kernels for 0%

commit v1 on v0

v1 whole, which is shorter than its diff:
```python
import functools

import jax
import jax.numpy as jnp
from jax import lax
from jax.experimental import pallas as pl
from jax.experimental.pallas import tpu as pltpu
from jax.sharding import PartitionSpec as P

MESH = pl.DeviceIdType.MESH
F32 = jnp.float32
BF16 = jnp.bfloat16
LANES = 128


def nt_dot(a, b):
    return lax.dot_general(a, b, (((1,), (1,)), ((), ())), preferred_element_type=F32)


def kernel(
    dims,
    fields_hbm, rows_ref, cols_ref, weight_ref, bias_ref, grad_hbm,
    stem_hbm, sums_ref,
    fields, above, side, side_in, corner_in, rows32, border, extra, spread, taps_b, diff,
    patches, band, acc, slope, stage, grads, grad_pre, corr, diag,
    part, part_in, xpart, xpart_in, zpart, zpart_in,
    load_sem, halo_send, halo_recv, grad_send, grad_recv, stem_send, stem_recv,
    part_send, part_recv, x_send, x_recv, z_send, z_recv,
):
    nx, ny, span, cin, cout, cap_x, cap_y, depth = dims
    half_x, half_y, half_z = cap_x // 2, cap_y // 2, depth // 2
    own = cout // ny
    planes = nx // span
    cy = cin * cap_y
    body = 9 * cy
    wide = patches.shape[0]
    cells = half_x * half_z

    gx, gy = lax.axis_index("gx"), lax.axis_index("gy")
    iz, ix = gx // span, gx % span

    def wrap(value, size):
        return lax.rem(value + size, size)

    def farthest_first(step):
        half = (step + 1) // 2
        return ny // 2 + jnp.where(step % 2 == 1, half, -half)

    def x_peer(d):
        return (iz * span + wrap(ix + d, span), gy)

    def z_peer(d):
        return (wrap(iz + d, planes) * span + ix, gy)

    barrier = pltpu.get_barrier_semaphore()

    def greet(device):
        pl.semaphore_signal(barrier, inc=1, device_id=device, device_id_type=MESH)

    def greet_y(step, carry):
        greet((gx, wrap(gy + farthest_first(step), ny)))
        return carry

    load = pltpu.make_async_copy(fields_hbm, fields, load_sem.at[0])
    load.start()
    mine = pltpu.make_async_copy(
        grad_hbm.at[:, :, pl.ds(gy * half_y, half_y), :],
        grads.at[pl.ds(gy * own, own)],
        load_sem.at[1],
    )
    mine.start()
    lax.fori_loop(0, ny - 1, greet_y, 0)
    for dx, dy in ((1, 0), (-1, 0), (1, 1), (-1, -1)):
        greet((wrap(gx + dx, nx), wrap(gy + dy, ny)))
    for d in range(1, span):
        greet(x_peer(d))
    for d in range(1, planes):
        greet(z_peer(d))
    pl.semaphore_wait(barrier, ny - 1 + 4 + span - 1 + planes - 1)

    def halo_copy(index, src, dst, dx, dy):
        return pltpu.make_async_remote_copy(
            src_ref=src, dst_ref=dst, send_sem=halo_send.at[index], recv_sem=halo_recv.at[index],
            device_id=(wrap(gx + dx, nx), wrap(gy + dy, ny)), device_id_type=MESH,
        )

    def grad_copy(d):
        to = wrap(gy + d, ny)
        return pltpu.make_async_remote_copy(
            src_ref=grad_hbm.at[:, :, pl.ds(to * half_y, half_y), :],
            dst_ref=grads.at[pl.ds(gy * own, own)],
            send_sem=grad_send.at[d], recv_sem=grad_recv.at[d],
            device_id=(gx, to), device_id_type=MESH,
        )

    load.wait()
    rows_out = halo_copy(0, fields.at[:, cap_x - 1], above, 1, 0)
    rows_out.start()
    for x in range(cap_x):
        for c in range(cin):
            tail = fields[c, x, cap_y - 16:cap_y, :].astype(F32)
            rows32[x * cin + c:x * cin + c + 1, :] = tail[15:16, :]
    side[...] = rows32[...].astype(BF16)
    side_out = halo_copy(1, side, side_in, 0, 1)
    side_out.start()
    corner_out = halo_copy(2, side, corner_in, 1, 1)
    corner_out.start()

    def start_grad(step, carry):
        grad_copy(farthest_first(step)).start()
        return carry

    lax.fori_loop(0, ny - 1, start_grad, 0)

    z_at = lax.broadcasted_iota(jnp.int32, (depth, 3 * half_z), 0)
    n_at = lax.broadcasted_iota(jnp.int32, (depth, 3 * half_z), 1)
    spread[...] = jnp.where(
        z_at == 2 * (n_at % half_z) - 1 + n_at // half_z, 1.0, 0.0
    ).astype(BF16)

    n_row = lax.broadcasted_iota(jnp.int32, (1, wide), 1)
    tail_at = n_row - body
    in_body = tail_at < 0
    in_edge = (tail_at >= 0) & (tail_at < 9 * cin)
    ones_at = tail_at == 9 * cin
    chan = jnp.where(in_body, (n_row // cap_y) % cin, tail_at % cin)
    off = jnp.where(in_body, n_row // cy, tail_at // cin)
    off_x, off_z = off // 3, off % 3
    first_tap = chan * 27 + off_x * 9 + off_z
    ext_y = jnp.where(in_body, n_row % cap_y + 1, jnp.where(in_edge, 0, -1000))
    w_at = lax.broadcasted_iota(jnp.int32, (LANES, wide), 0)
    for b in range(3):
        goal = jnp.where(in_body | in_edge, first_tap + 3 * b, -1)
        if b == 0:
            goal = jnp.where(ones_at, cin * 27, goal)
        taps_b[b] = jnp.where(w_at == goal, 1.0, 0.0).astype(BF16)
    q_at = lax.broadcasted_iota(jnp.int32, (half_y, wide), 0)
    diff[...] = jnp.where(ones_at, 0, ext_y - 2 * q_at)

    for b in range(3):
        corr[b] = jnp.dot(weight_ref[...], taps_b[b, 0:cin * 27, :], preferred_element_type=F32)

    def fill_band(o, carry):
        rows = pl.ds(pl.multiple_of(o * half_y, half_y), half_y)
        value = jnp.zeros((half_y, wide), F32)
        for b in range(3):
            value = jnp.where(diff[...] == b, corr[b, pl.ds(o, 1), :], value)
        band[rows, :] = value.astype(BF16)
        return carry

    lax.fori_loop(0, cout, fill_band, 0)

    rows_out.wait_recv()
    side_out.wait_recv()
    corner_out.wait_recv()
    edge_x = cap_x - rows_ref[gx]
    edge_y = cap_y - cols_ref[gy]
    inner_x = gx > 0
    inner_y = gy > 0
    rows32[...] = side_in[...].astype(F32)
    border[...] = jnp.zeros_like(border)
    corner = corner_in[cin * cap_x - 16:cin * cap_x, :].astype(F32)[16 - cin:16, :]
    for x in range(cap_x + 1):
        line = jnp.where((x == edge_x) & inner_x & inner_y, corner, 0.0)
        if x > 0:
            line = jnp.where((x > edge_x) & inner_y, rows32[(x - 1) * cin:x * cin, :], line)
        border[x * cin:(x + 1) * cin, :] = line
    y_at = lax.broadcasted_iota(jnp.int32, (cap_y, depth), 0) + 1
    for x in range(cap_x + 1):
        blocks = []
        for c in range(cin):
            block = jnp.where((x == edge_x) & inner_x, above[c].astype(F32), 0.0)
            if x > 0:
                block = jnp.where(x > edge_x, fields[c, x - 1].astype(F32), block)
            line = border[x * cin + c:x * cin + c + 1, :]
            block = jnp.where(y_at > edge_y, block, jnp.where(y_at == edge_y, line, 0.0))
            blocks.append(block.astype(BF16))
        split = jnp.dot(
            jnp.concatenate(blocks, axis=0), spread[...], preferred_element_type=F32
        ).astype(BF16)
        for a in range(3):
            if (x - a) % 2 == 0 and 0 <= (x - a) // 2 < half_x:
                p = (x - a) // 2
                for k in range(3):
                    row = (a * 3 + k) * cy
                    patches[row:row + cy, p * half_z:(p + 1) * half_z] = split[:, k * half_z:(k + 1) * half_z]
    before = jnp.where(edge_y == 0, border[...], 0.0).astype(BF16)
    split = jnp.dot(before, spread[...], preferred_element_type=F32)
    extra[...] = jnp.zeros_like(extra)
    for a in range(3):
        for p in range(half_x):
            x = 2 * p + a
            for k in range(3):
                row = (a * 3 + k) * cin
                extra[row:row + cin, p * half_z:(p + 1) * half_z] = (
                    split[x * cin:(x + 1) * cin, k * half_z:(k + 1) * half_z]
                )
    extra[9 * cin:9 * cin + 1, :] = jnp.ones((1, cells), F32)
    patches[body:wide, :] = extra[...].astype(BF16)

    half_rows = cout * half_y // 2

    def multiply(m, carry):
        rows = pl.ds(pl.multiple_of(m * half_rows, half_rows), half_rows)
        acc[rows, :] = jnp.dot(band[rows, :], patches[...], preferred_element_type=F32)
        return carry

    lax.fori_loop(0, 2, multiply, 0)
    q_cell = lax.broadcasted_iota(jnp.int32, (half_y, cells), 0)
    p_cell = lax.broadcasted_iota(jnp.int32, (half_y, cells), 1) // half_z
    live = (2 * q_cell >= edge_y) & (2 * p_cell >= edge_x)

    def stem_copy(d):
        to = wrap(gy + d, ny)
        return pltpu.make_async_remote_copy(
            src_ref=stage.at[pl.ds(to * own, own)],
            dst_ref=stem_hbm.at[:, :, pl.ds(gy * half_y, half_y), :],
            send_sem=stem_send.at[d], recv_sem=stem_recv.at[d],
            device_id=(gx, to), device_id_type=MESH,
        )

    def activate(o):
        rows = pl.ds(pl.multiple_of(o * half_y, half_y), half_y)
        pre = jnp.where(live, acc[rows, :] + bias_ref[o], 0.0).astype(BF16).astype(F32)
        sigma = 1.0 / (1.0 + jnp.exp(-pre))
        value = (pre * sigma).astype(BF16)
        slope[rows, :] = jnp.where(live, sigma * (1.0 + pre * (1.0 - sigma)), 0.0)
        for p in range(half_x):
            stage[o, p] = value[:, p * half_z:(p + 1) * half_z]

    def forward(step, carry):
        d = farthest_first(step)
        for part_of in range(own):
            activate(wrap(gy + d, ny) * own + part_of)
        stem_copy(d).start()
        return carry

    lax.fori_loop(0, ny - 1, forward, 0)
    for part_of in range(own):
        activate(gy * own + part_of)
    keep = pltpu.make_async_copy(
        stage.at[pl.ds(gy * own, own)],
        stem_hbm.at[:, :, pl.ds(gy * half_y, half_y), :],
        load_sem.at[2],
    )
    keep.start()

    mine.wait()

    def wait_grad(d, carry):
        grad_copy(d).wait_recv()
        return carry

    lax.fori_loop(1, ny, wait_grad, 0)

    def chain(o, carry):
        rows = pl.ds(pl.multiple_of(o * half_y, half_y), half_y)
        for p in range(half_x):
            lanes = slice(p * half_z, (p + 1) * half_z)
            grad_pre[rows, lanes] = (grads[o, p].astype(F32) * slope[rows, lanes]).astype(BF16)
        return carry

    lax.fori_loop(0, cout, chain, 0)

    group = diag.shape[0] // half_y

    def correlate(m, carry):
        rows = pl.ds(pl.multiple_of(m * group * half_y, group * half_y), group * half_y)
        diag[...] = nt_dot(grad_pre[rows, :], patches[...])

        def pick(i, inner):
            value = diag[pl.ds(pl.multiple_of(i * half_y, half_y), half_y), :]
            for b in range(3):
                corr[b, pl.ds(m * group + i, 1), :] = jnp.sum(
                    jnp.where(diff[...] == b, value, 0.0), axis=0, keepdims=True
                )
            return inner

        return lax.fori_loop(0, group, pick, carry)

    lax.fori_loop(0, cout // group, correlate, 0)
    total = jnp.zeros((cout, LANES), F32)
    for b in range(3):
        high = corr[b].astype(BF16)
        low = (corr[b] - high.astype(F32)).astype(BF16)
        total = total + (nt_dot(high, taps_b[b]) + nt_dot(low, taps_b[b]))

    part[...] = jnp.zeros_like(part)
    for j in range(ny):
        part[j, 0:own, :] = total[j * own:(j + 1) * own, :]

    def part_copy(d):
        to = wrap(gy + d, ny)
        return pltpu.make_async_remote_copy(
            src_ref=part.at[to], dst_ref=part_in.at[d],
            send_sem=part_send.at[d], recv_sem=part_recv.at[d],
            device_id=(gx, to), device_id_type=MESH,
        )

    def start_part(step, carry):
        part_copy(farthest_first(step)).start()
        return carry

    lax.fori_loop(0, ny - 1, start_part, 0)

    def take_part(d, held):
        part_copy(d).wait_recv()
        return held + part_in[d]

    xpart[...] = lax.fori_loop(1, ny, take_part, part[gy])

    def x_copy(d):
        return pltpu.make_async_remote_copy(
            src_ref=xpart, dst_ref=xpart_in.at[ix],
            send_sem=x_send.at[d], recv_sem=x_recv.at[d],
            device_id=x_peer(d), device_id_type=MESH,
        )

    def z_copy(d):
        return pltpu.make_async_remote_copy(
            src_ref=zpart, dst_ref=zpart_in.at[iz],
            send_sem=z_send.at[d], recv_sem=z_recv.at[d],
            device_id=z_peer(d), device_id_type=MESH,
        )

    for d in range(1, span):
        x_copy(d).start()
    xpart_in[ix] = xpart[...]
    for d in range(1, span):
        x_copy(d).wait_recv()
    zpart[...] = sum([xpart_in[i] for i in range(1, span)], xpart_in[0])
    for d in range(1, planes):
        z_copy(d).start()
    zpart_in[iz] = zpart[...]
    for d in range(1, planes):
        z_copy(d).wait_recv()
    sums_ref[...] = sum([zpart_in[i] for i in range(1, planes)], zpart_in[0])

    def finish(d, carry):
        stem_copy(d).wait_recv()
        stem_copy(d).wait_send()
        grad_copy(d).wait_send()
        part_copy(d).wait_send()
        return carry

    lax.fori_loop(1, ny, finish, 0)
    for d in range(1, span):
        x_copy(d).wait_send()
    for d in range(1, planes):
        z_copy(d).wait_send()
    rows_out.wait_send()
    side_out.wait_send()
    corner_out.wait_send()
    keep.wait()


def local(nx, ny, span, fields, rows_live, cols_live, weight, bias, grad_out):
    cin, cap_x, cap_y, depth = fields.shape
    cout = weight.shape[0]
    half_x, half_y, half_z = cap_x // 2, cap_y // 2, depth // 2
    planes = nx // span
    cells = half_x * half_z
    cy = cin * cap_y
    wide = 9 * cy + LANES
    dims = (nx, ny, span, cin, cout, cap_x, cap_y, depth)
    vmem = pl.BlockSpec(memory_space=pltpu.VMEM)
    smem = pl.BlockSpec(memory_space=pltpu.SMEM)
    hbm = pl.BlockSpec(memory_space=pl.ANY)
    dma = pltpu.SemaphoreType.DMA
    stem, sums = pl.pallas_call(
        functools.partial(kernel, dims),
        out_shape=(
            jax.ShapeDtypeStruct(grad_out.shape, BF16),
            jax.ShapeDtypeStruct((8, LANES), F32),
        ),
        in_specs=[hbm, smem, smem, vmem, smem, hbm],
        out_specs=(hbm, vmem),
        scratch_shapes=[
            pltpu.VMEM((cin, cap_x, cap_y, depth), BF16),
            pltpu.VMEM((cin, cap_y, depth), BF16),
            pltpu.VMEM((cin * cap_x, depth), BF16),
            pltpu.VMEM((cin * cap_x, depth), BF16),
            pltpu.VMEM((cin * cap_x, depth), BF16),
            pltpu.VMEM((cin * cap_x, depth), F32),
            pltpu.VMEM((48, depth), F32),
            pltpu.VMEM((LANES, cells), F32),
            pltpu.VMEM((depth, 3 * half_z), BF16),
            pltpu.VMEM((3, LANES, wide), BF16),
            pltpu.VMEM((half_y, wide), jnp.int32),
            pltpu.VMEM((wide, cells), BF16),
            pltpu.VMEM((cout * half_y, wide), BF16),
            pltpu.VMEM((cout * half_y, cells), F32),
            pltpu.VMEM((cout * half_y, cells), F32),
            pltpu.VMEM((cout, half_x, half_y, half_z), BF16),
            pltpu.VMEM((cout, half_x, half_y, half_z), BF16),
            pltpu.VMEM((cout * half_y, cells), BF16),
            pltpu.VMEM((3, cout, wide), F32),
            pltpu.VMEM((8 * half_y, wide), F32),
            pltpu.VMEM((ny, 8, LANES), F32),
            pltpu.VMEM((ny, 8, LANES), F32),
            pltpu.VMEM((8, LANES), F32),
            pltpu.VMEM((span, 8, LANES), F32),
            pltpu.VMEM((8, LANES), F32),
            pltpu.VMEM((planes, 8, LANES), F32),
            dma((3,)), dma((3,)), dma((3,)),
            dma((ny,)), dma((ny,)), dma((ny,)), dma((ny,)), dma((ny,)), dma((ny,)),
            dma((span,)), dma((span,)), dma((planes,)), dma((planes,)),
        ],
        compiler_params=pltpu.CompilerParams(
            collective_id=0, has_side_effects=True, vmem_limit_bytes=40 * 1024 * 1024
        ),
    )(fields, rows_live, cols_live, weight, bias, grad_out)
    own = cout // ny
    taps = weight.shape[1]
    return stem, sums[:own, :taps], sums[:own, taps]


def solution(mesh):
    nx, ny = mesh.shape["gx"], mesh.shape["gy"]
    span = 4 if nx % 4 == 0 else 1
    in_specs = (P(None, "gx", "gy", None), P(), P(), P(), P(), P("gy", "gx", None, None))
    out_specs = (P("gy", "gx", None, None), P("gy", None), P("gy"))
    run = functools.partial(local, nx, ny, span)
    return jax.shard_map(run, mesh=mesh, in_specs=in_specs, out_specs=out_specs, check_vma=False)
```

time: 273 us -> 60.4 us (0.22)
  the two profiles are of different devices: /device:TPU:2 before, /device:TPU:1 now
where the time goes in v1:
time: 60.4 us; the launch traced here: 60.2 us
  Pallas kernels  52.7 us (87%)
  local copies, waits for them, and re-layouts  6.79 us (11%)
  between operations  0.65 us (1%)
    pallas_call x1, Pallas kernels, local(): pl.pallas_call(functools.partial(kernel, dims), out_shape=(jax.ShapeDtype...  52.7 us
    unnamed x13, local copies, waits for them, and re-layouts  5.53 us
    slice x2, local copies, waits for them, and re-layouts, local(): return (stem, sums[:own, :taps], sums[:own, taps])  1.26 us

profile of v1, /device:TPU:1, one launch (start us, length us, event | category | flops | bytes accessed | tf_op | source)
XLA Modules:
  0.0 60.2 jit_solution(12775122516450406043)
XLA Ops:
  0.6 0.0 copy-start
  0.6 1.0 %copy-done = bf16[4,8,32,256]{3,2,1,0:T(8,128)(2,1)S(1)} copy-done((bf16[4,8,32,256]{3,2,1,0:T(8,128)(2,1)S(1)}, bf16[4,8,32,256]{3,2,1,0:T(8,128)(2,1)}, u32[]{:S(2)}) %copy-start) | copy-done | bytes 524312
  1.7 0.0 copy-start.1
  1.7 1.0 %copy-done.1 = bf16[2,4,256,128]{3,2,1,0:T(8,128)(2,1)S(1)} copy-done((bf16[2,4,256,128]{3,2,1,0:T(8,128)(2,1)S(1)}, bf16[2,4,256,128]{3,2,1,0:T(8,128)(2,1)}, u32[]{:S(2)}) %copy-start.1) | copy-done | bytes 524312
  2.7 0.0 copy-start.2
  2.7 0.7 %copy-done.2 = bf16[32,108]{1,0:T(8,128)(2,1)S(1)} copy-done((bf16[32,108]{1,0:T(8,128)(2,1)S(1)}, bf16[32,108]{1,0:T(8,128)(2,1)}, u32[]{:S(2)}) %copy-start.2) | copy-done | bytes 6936
  3.4 0.0 copy-start.3
  3.4 0.7 %copy-done.3 = s32[32]{0:T(128)S(1)} copy-done((s32[32]{0:T(128)S(1)}, s32[32]{0:T(128)}, u32[]{:S(2)}) %copy-start.3) | copy-done | bytes 152
  4.1 0.0 copy-start.4
  4.1 0.7 %copy-done.4 = s32[16]{0:T(128)S(1)} copy-done((s32[16]{0:T(128)S(1)}, s32[16]{0:T(128)}, u32[]{:S(2)}) %copy-start.4) | copy-done | bytes 88
  4.7 0.0 copy-start.5
  4.7 0.7 %copy-done.5 = f32[32]{0:T(128)S(1)} copy-done((f32[32]{0:T(128)S(1)}, f32[32]{0:T(128)}, u32[]{:S(2)}) %copy-start.5) | copy-done | bytes 152
  5.4 52.7 %shard_map.85 = (bf16[2,4,256,128]{3,2,1,0:T(8,128)(2,1)S(1)}, f32[8,128]{1,0:T(8,128)S(1)}) custom-call(bf16[4,8,32,256]{3,2,1,0:T(8,128)(2,1)S(1)} %copy-done, s32[32]{0:T(128)S(1)} %copy-done.3, s32[16]{0:T(128)S(1)} %copy-done.4, bf16[32,108]{1,0:T(8,128)(2,1)S(1)} %copy-done.2, f32[32]{0:T(128)S(1)} %copy-done.5, bf16[2,4,256,128]{3,2,1,0:T(8,128)(2,1)S(1)} %copy-done.1), custom_call_target="tpu_custom_call" | custom-call | tf_op jit(solution)/shard_map/pallas_call | solution.py:370
  58.1 0.6 slice.6
  58.7 0.7 %slice_reduce_fusion = f32[2]{0:T(128)} fusion(f32[8,128]{1,0:T(8,128)S(1)} %get-tuple-element.6), kind=kLoop, calls=%fused_computation | loop fusion | bytes 16 | tf_op jit(solution)/shard_map/slice | solution.py:415
  59.4 0.8 %copy.10 = bf16[2,4,256,128]{3,2,1,0:T(8,128)(2,1)} copy(bf16[2,4,256,128]{3,2,1,0:T(8,128)(2,1)S(1)} %get-tuple-element.10) | data formatting | bytes 1048576
Async XLA Ops:
  0.6 1.0 %copy-start = (bf16[4,8,32,256]{3,2,1,0:T(8,128)(2,1)S(1)}, bf16[4,8,32,256]{3,2,1,0:T(8,128)(2,1)}, u32[]{:S(2)}) copy-start(bf16[4,8,32,256]{3,2,1,0:T(8,128)(2,1)} %fields_hbm.1) | copy-start | bytes 1572868
  1.7 1.0 %copy-start.1 = (bf16[2,4,256,128]{3,2,1,0:T(8,128)(2,1)S(1)}, bf16[2,4,256,128]{3,2,1,0:T(8,128)(2,1)}, u32[]{:S(2)}) copy-start(bf16[2,4,256,128]{3,2,1,0:T(8,128)(2,1)} %grad_hbm.1) | copy-start | bytes 1572868
  2.7 0.7 %copy-start.2 = (bf16[32,108]{1,0:T(8,128)(2,1)S(1)}, bf16[32,108]{1,0:T(8,128)(2,1)}, u32[]{:S(2)}) copy-start(bf16[32,108]{1,0:T(8,128)(2,1)} %weight_ref.1) | copy-start | bytes 20740
  3.4 0.7 %copy-start.3 = (s32[32]{0:T(128)S(1)}, s32[32]{0:T(128)}, u32[]{:S(2)}) copy-start(s32[32]{0:T(128)} %rows_ref.1) | copy-start | bytes 388
  4.1 0.7 %copy-start.4 = (s32[16]{0:T(128)S(1)}, s32[16]{0:T(128)}, u32[]{:S(2)}) copy-start(s32[16]{0:T(128)} %cols_ref.1) | copy-start | bytes 196
  4.7 0.7 %copy-start.5 = (f32[32]{0:T(128)S(1)}, f32[32]{0:T(128)}, u32[]{:S(2)}) copy-start(f32[32]{0:T(128)} %bias_ref.1) | copy-start | bytes 388

commit v2 on v1

v2 whole, which is shorter than its diff:
```python
import functools

import jax
import jax.numpy as jnp
from jax import lax
from jax.experimental import pallas as pl
from jax.experimental.pallas import tpu as pltpu
from jax.sharding import PartitionSpec as P

MESH = pl.DeviceIdType.MESH
F32 = jnp.float32
BF16 = jnp.bfloat16
LANES = 128
EARLY = 0
SOON = 1
FIRST = 6
GROUP = 4


def nt_dot(a, b):
    return lax.dot_general(a, b, (((1,), (1,)), ((), ())), preferred_element_type=F32)


def kernel(
    dims,
    fields_hbm, rows_hbm, cols_hbm, weight_hbm, bias_hbm, grad_hbm,
    stem_hbm, sums_ref,
    rows_ref, cols_ref, weight_ref, bias_ref, fields, above, side, side_in, corner_in,
    rows32, lines, border, spread, taps_b, band, patches, acc, slope, stage, grads, grad_pre,
    part, part_in, xpart, xpart_in, zpart, zpart_in,
    load_sem, halo_send, halo_recv, grad_send, grad_recv, stem_send, stem_recv,
    part_send, part_recv, x_send, x_recv, z_send, z_recv,
):
    nx, ny, span, cin, cout, cap_x, cap_y, depth = dims
    half_x, half_y, half_z = cap_x // 2, cap_y // 2, depth // 2
    own = cout // ny
    planes = nx // span
    own = cout // ny
    cells = half_x * half_z
    tall = patches.shape[1]
    window = band.shape[1] // 9
    reach = half_y // GROUP

    gx, gy = lax.axis_index("gx"), lax.axis_index("gy")
    iz, ix = gx // span, gx % span

    def wrap(value, size):
        return lax.rem(value + size, size)

    def farthest_first(step):
        half = (step + 1) // 2
        return ny // 2 + jnp.where(step % 2 == 1, half, -half)

    def x_peer(d):
        return (iz * span + wrap(ix + d, span), gy)

    def z_peer(d):
        return (wrap(iz + d, planes) * span + ix, gy)

    barrier = pltpu.get_barrier_semaphore()

    def greet(device):
        pl.semaphore_signal(barrier, inc=1, device_id=device, device_id_type=MESH)

    def greet_y(step, carry):
        greet((gx, wrap(gy + farthest_first(step), ny)))
        return carry

    load = pltpu.make_async_copy(fields_hbm, fields, load_sem.at[0])
    load.start()
    mine = pltpu.make_async_copy(
        grad_hbm.at[:, :, pl.ds(gy * half_y, half_y), :],
        grads.at[pl.ds(gy * own, own)],
        load_sem.at[1],
    )
    mine.start()
    small = [
        pltpu.make_async_copy(src, dst, load_sem.at[3 + i])
        for i, (src, dst) in enumerate(
            ((rows_hbm, rows_ref), (cols_hbm, cols_ref), (weight_hbm, weight_ref), (bias_hbm, bias_ref))
        )
    ]
    for copy in small:
        copy.start()
    lax.fori_loop(0, ny - 1, greet_y, 0)
    for dx, dy in ((1, 0), (-1, 0), (1, 1), (-1, -1)):
        greet((wrap(gx + dx, nx), wrap(gy + dy, ny)))
    for d in range(1, span):
        greet(x_peer(d))
    for d in range(1, planes):
        greet(z_peer(d))
    pl.semaphore_wait(barrier, ny - 1 + 4 + span - 1 + planes - 1)

    def halo_copy(index, src, dst, dx, dy):
        return pltpu.make_async_remote_copy(
            src_ref=src, dst_ref=dst, send_sem=halo_send.at[index], recv_sem=halo_recv.at[index],
            device_id=(wrap(gx + dx, nx), wrap(gy + dy, ny)), device_id_type=MESH,
        )

    def grad_copy(d):
        to = wrap(gy + d, ny)
        return pltpu.make_async_remote_copy(
            src_ref=grad_hbm.at[:, :, pl.ds(to * half_y, half_y), :],
            dst_ref=grads.at[pl.ds(gy * own, own)],
            send_sem=grad_send.at[d], recv_sem=grad_recv.at[d],
            device_id=(gx, to), device_id_type=MESH,
        )

    def start_grad(step, carry):
        grad_copy(farthest_first(step)).start()
        return carry

    rows_out = halo_copy(0, fields_hbm.at[:, cap_x - 1], above, 1, 0)
    rows_out.start()
    lax.fori_loop(0, min(FIRST, ny - 1), start_grad, 0)

    load.wait()
    for x in range(cap_x):
        for c in range(cin):
            for h in range(2):
                lines[x + 1, h, pl.ds(cin + c, cap_y, stride=cin), :] = (
                    fields[c, x, :, h * half_z:(h + 1) * half_z].astype(F32)
                )
        for h in range(2):
            rows32[x * cin:(x + 1) * cin, h * half_z:(h + 1) * half_z] = (
                lines[x + 1, h, cin * cap_y:cin * (cap_y + 1), :]
            )
    side[...] = rows32[...].astype(BF16)
    side_out = halo_copy(1, side, side_in, 0, 1)
    side_out.start()
    corner_out = halo_copy(2, side, corner_in, 1, 1)
    corner_out.start()
    lax.fori_loop(min(FIRST, ny - 1), ny - 1, start_grad, 0)

    z_at = lax.broadcasted_iota(jnp.int32, (depth, 3 * half_z), 0)
    n_at = lax.broadcasted_iota(jnp.int32, (depth, 3 * half_z), 1)
    spread[...] = jnp.where(
        z_at == 2 * (n_at % half_z) - 1 + n_at // half_z, 1.0, 0.0
    ).astype(BF16)

    n_row = lax.broadcasted_iota(jnp.int32, (1, 9 * window), 1)
    off, place = n_row // window, n_row % window
    first_tap = (place % cin) * 27 + (off // 3) * 9 + off % 3
    ext_y = place // cin
    w_at = lax.broadcasted_iota(jnp.int32, (LANES, 9 * window), 0)
    for b in range(3):
        taps_b[b] = jnp.where(w_at == first_tap + 3 * b, 1.0, 0.0).astype(BF16)
    for copy in small:
        copy.wait()

    by_tap = [
        jnp.dot(weight_ref[...], taps_b[b, 0:cin * 27, :], preferred_element_type=F32)
        for b in range(3)
    ]
    for i in range(GROUP):
        value = jnp.zeros((cout, 9 * window), F32)
        for b in range(3):
            value = jnp.where(ext_y == 2 * i + b, by_tap[b], value)
        band[i * cout:(i + 1) * cout, :] = value.astype(BF16)

    rows_out.wait_recv()
    side_out.wait_recv()
    corner_out.wait_recv()
    edge_x = cap_x - rows_ref[gx]
    edge_y = cap_y - cols_ref[gy]
    inner_x = gx > 0
    inner_y = gy > 0
    rows32[...] = side_in[...].astype(F32)
    corner = corner_in[cin * cap_x - 16:cin * cap_x, :].astype(F32)[16 - cin:16, :]
    for x in range(cap_x + 1):
        line = jnp.where((x == edge_x) & inner_x & inner_y, corner, 0.0)
        if x > 0:
            line = jnp.where((x > edge_x) & inner_y, rows32[(x - 1) * cin:x * cin, :], line)
        for i in range(8 // cin):
            border[x, i * cin:(i + 1) * cin, :] = line
    for c in range(cin):
        for h in range(2):
            lines[0, h, pl.ds(cin + c, cap_y, stride=cin), :] = (
                above[c, :, h * half_z:(h + 1) * half_z].astype(F32)
            )
    whole = (tall // 8, 8, half_z)
    y_at = (
        lax.broadcasted_iota(jnp.int32, whole, 0) * 8 + lax.broadcasted_iota(jnp.int32, whole, 1)
    ) // cin
    inside = (y_at > edge_y) & (y_at <= cap_y)
    at_edge = y_at == edge_y
    for x in range(cap_x + 1):
        halves = []
        for h in range(2):
            value = jnp.where((x == edge_x) & inner_x, lines[0, h], 0.0)
            if x > 0:
                value = jnp.where(x > edge_x, lines[x, h], value)
            line = border[x, :, h * half_z:(h + 1) * half_z][None]
            value = jnp.where(inside, value.reshape(whole), jnp.where(at_edge, line, 0.0))
            halves.append(value.reshape(tall, half_z).astype(BF16))
        value = jnp.concatenate(halves, axis=1)
        split = jnp.dot(
            value, spread[...], preferred_element_type=F32
        ).astype(BF16)
        for a in range(3):
            if (x - a) % 2 == 0 and 0 <= (x - a) // 2 < half_x:
                p = (x - a) // 2
                for k in range(3):
                    patches[a * 3 + k, :, p * half_z:(p + 1) * half_z] = (
                        split[:, k * half_z:(k + 1) * half_z]
                    )

    def windows(m):
        first = 2 * GROUP * cin * m
        return patches[:, first:first + window, :].reshape(9 * window, cells)

    for m in range(reach):
        value = jnp.dot(band[...], windows(m), preferred_element_type=F32)
        for i in range(GROUP):
            for p in range(half_x):
                acc[p, pl.ds(m * GROUP + i, cout, stride=half_y), :] = (
                    value[i * cout:(i + 1) * cout, p * half_z:(p + 1) * half_z]
                )
    q_live = 2 * lax.broadcasted_iota(jnp.int32, (half_y, half_z), 0) >= edge_y

    def stem_copy(d):
        to = wrap(gy + d, ny)
        return pltpu.make_async_remote_copy(
            src_ref=stage.at[pl.ds(to * own, own)],
            dst_ref=stem_hbm.at[:, :, pl.ds(gy * half_y, half_y), :],
            send_sem=stem_send.at[d], recv_sem=stem_recv.at[d],
            device_id=(gx, to), device_id_type=MESH,
        )

    def activate(o):
        rows = pl.ds(pl.multiple_of(o * half_y, half_y), half_y)
        for p in range(half_x):
            live = q_live & (2 * p >= edge_x)
            pre = jnp.where(live, acc[p, rows, :] + bias_ref[o], 0.0).astype(BF16).astype(F32)
            sigma = 1.0 / (1.0 + jnp.exp(-pre))
            stage[o, p] = (pre * sigma).astype(BF16)
            slope[p, rows, :] = jnp.where(live, sigma * (1.0 + pre * (1.0 - sigma)), 0.0)

    def forward(step, carry):
        d = farthest_first(step)
        for part_of in range(own):
            activate(wrap(gy + d, ny) * own + part_of)
        return carry

    def start_stem(step, carry):
        stem_copy(farthest_first(step)).start()
        return carry

    lax.fori_loop(0, ny - 1, forward, 0)
    for part_of in range(own):
        activate(gy * own + part_of)
    lax.fori_loop(0, min(EARLY, ny - 1), start_stem, 0)
    keep = pltpu.make_async_copy(
        stage.at[pl.ds(gy * own, own)],
        stem_hbm.at[:, :, pl.ds(gy * half_y, half_y), :],
        load_sem.at[2],
    )
    keep.start()

    mine.wait()

    def wait_grad(d, carry):
        grad_copy(d).wait_recv()
        return carry

    lax.fori_loop(1, ny, wait_grad, 0)
    lax.fori_loop(min(EARLY, ny - 1), min(SOON, ny - 1), start_stem, 0)

    def chain(o, carry):
        rows = pl.ds(pl.multiple_of(o * half_y, half_y), half_y)
        for p in range(half_x):
            value = (grads[o, p].astype(F32) * slope[p, rows, :]).astype(BF16)
            grad_pre[p, rows, :] = value.astype(F32)
        return carry

    lax.fori_loop(0, cout, chain, 0)

    corr = jnp.zeros((GROUP * cout, 9 * window), F32)
    bias_sum = jnp.zeros((cout, cells), F32)
    for m in range(reach):
        values = [
            jnp.concatenate(
                [
                    grad_pre[p, pl.ds(m * GROUP + i, cout, stride=half_y), :]
                    for p in range(half_x)
                ],
                axis=1,
            )
            for i in range(GROUP)
        ]
        bias_sum = bias_sum + sum(values[1:], values[0])
        corr = corr + nt_dot(jnp.concatenate(values, axis=0).astype(BF16), windows(m))
    total = jnp.zeros((cout, LANES), F32)
    for b in range(3):
        picked = jnp.zeros((cout, 9 * window), F32)
        for i in range(GROUP):
            picked = jnp.where(ext_y == 2 * i + b, corr[i * cout:(i + 1) * cout, :], picked)
        high = picked.astype(BF16)
        low = (picked - high.astype(F32)).astype(BF16)
        total = total + (nt_dot(high, taps_b[b]) + nt_dot(low, taps_b[b]))
    lane = lax.broadcasted_iota(jnp.int32, (cout, LANES), 1)
    total = jnp.where(lane == cin * 27, jnp.sum(bias_sum, axis=1, keepdims=True), total)

    for j in range(ny):
        part[j] = total[j * own:(j + 1) * own, :]

    def part_copy(d):
        to = wrap(gy + d, ny)
        return pltpu.make_async_remote_copy(
            src_ref=part.at[to], dst_ref=part_in.at[d],
            send_sem=part_send.at[d], recv_sem=part_recv.at[d],
            device_id=(gx, to), device_id_type=MESH,
        )

    def start_part(step, carry):
        part_copy(farthest_first(step)).start()
        return carry

    lax.fori_loop(0, ny - 1, start_part, 0)
    lax.fori_loop(min(SOON, ny - 1), ny - 1, start_stem, 0)

    def take_part(d, held):
        part_copy(d).wait_recv()
        return held + part_in[d]

    xpart[...] = lax.fori_loop(1, ny, take_part, part[gy])

    def x_copy(d):
        return pltpu.make_async_remote_copy(
            src_ref=xpart, dst_ref=xpart_in.at[ix],
            send_sem=x_send.at[d], recv_sem=x_recv.at[d],
            device_id=x_peer(d), device_id_type=MESH,
        )

    def z_copy(d):
        return pltpu.make_async_remote_copy(
            src_ref=zpart, dst_ref=zpart_in.at[iz],
            send_sem=z_send.at[d], recv_sem=z_recv.at[d],
            device_id=z_peer(d), device_id_type=MESH,
        )

    for d in range(1, span):
        x_copy(d).start()
    xpart_in[ix] = xpart[...]
    for d in range(1, span):
        x_copy(d).wait_recv()
    zpart[...] = sum([xpart_in[i] for i in range(1, span)], xpart_in[0])
    for d in range(1, planes):
        z_copy(d).start()
    zpart_in[iz] = zpart[...]
    for d in range(1, planes):
        z_copy(d).wait_recv()
    sums_ref[...] = sum([zpart_in[i] for i in range(1, planes)], zpart_in[0])

    def finish(d, carry):
        stem_copy(d).wait_recv()
        stem_copy(d).wait_send()
        grad_copy(d).wait_send()
        part_copy(d).wait_send()
        return carry

    lax.fori_loop(1, ny, finish, 0)
    for d in range(1, span):
        x_copy(d).wait_send()
    for d in range(1, planes):
        z_copy(d).wait_send()
    rows_out.wait_send()
    side_out.wait_send()
    corner_out.wait_send()
    keep.wait()


def hand_over(own, taps, landed, sums, stem, weight_grad, bias_grad, scalars, sem):
    out = pltpu.make_async_copy(landed, stem, sem.at[0])
    out.start()
    read = pltpu.make_async_copy(sums, scalars, sem.at[1])
    read.start()
    weight_grad[...] = sums[0:own, 0:taps]
    read.wait()
    for i in range(own):
        bias_grad[i] = scalars[i, taps]
    out.wait()


def local(nx, ny, span, fields, rows_live, cols_live, weight, bias, grad_out):
    cin, cap_x, cap_y, depth = fields.shape
    cout = weight.shape[0]
    half_x, half_y, half_z = cap_x // 2, cap_y // 2, depth // 2
    planes = nx // span
    own = cout // ny
    cells = half_x * half_z
    tall = cin * (cap_y + 4)
    window = -(-(2 * GROUP + 1) * cin // 16) * 16
    dims = (nx, ny, span, cin, cout, cap_x, cap_y, depth)
    vmem = pl.BlockSpec(memory_space=pltpu.VMEM)
    hbm = pl.BlockSpec(memory_space=pl.ANY)
    dma = pltpu.SemaphoreType.DMA
    landed, sums = pl.pallas_call(
        functools.partial(kernel, dims),
        out_shape=(
            pltpu.VMEM(grad_out.shape, BF16),
            pltpu.VMEM((own, LANES), F32),
        ),
        in_specs=[hbm] * 6,
        out_specs=(vmem, vmem),
        scratch_shapes=[
            pltpu.SMEM(rows_live.shape, jnp.int32),
            pltpu.SMEM(cols_live.shape, jnp.int32),
            pltpu.VMEM(weight.shape, BF16),
            pltpu.SMEM(bias.shape, F32),
            pltpu.VMEM((cin, cap_x, cap_y, depth), BF16),
            pltpu.VMEM((cin, cap_y, depth), BF16),
            pltpu.VMEM((cin * cap_x, depth), BF16),
            pltpu.VMEM((cin * cap_x, depth), BF16),
            pltpu.VMEM((cin * cap_x, depth), BF16),
            pltpu.VMEM((cin * cap_x, depth), F32),
            pltpu.VMEM((cap_x + 1, 2, tall, half_z), F32),
            pltpu.VMEM((cap_x + 1, 8, depth), F32),
            pltpu.VMEM((depth, 3 * half_z), BF16),
            pltpu.VMEM((3, LANES, 9 * window), BF16),
            pltpu.VMEM((GROUP * cout, 9 * window), BF16),
            pltpu.VMEM((9, tall, cells), BF16),
            pltpu.VMEM((half_x, cout * half_y, half_z), F32),
            pltpu.VMEM((half_x, cout * half_y, half_z), F32),
            pltpu.VMEM((cout, half_x, half_y, half_z), BF16),
            pltpu.VMEM((cout, half_x, half_y, half_z), BF16),
            pltpu.VMEM((half_x, cout * half_y, half_z), F32),
            pltpu.VMEM((ny, own, LANES), F32),
            pltpu.VMEM((ny, own, LANES), F32),
            pltpu.VMEM((own, LANES), F32),
            pltpu.VMEM((span, own, LANES), F32),
            pltpu.VMEM((own, LANES), F32),
            pltpu.VMEM((planes, own, LANES), F32),
            dma((7,)), dma((3,)), dma((3,)),
            dma((ny,)), dma((ny,)), dma((ny,)), dma((ny,)), dma((ny,)), dma((ny,)),
            dma((span,)), dma((span,)), dma((planes,)), dma((planes,)),
        ],
        compiler_params=pltpu.CompilerParams(
            collective_id=0, has_side_effects=True, vmem_limit_bytes=63 * 1024 * 1024
        ),
    )(fields, rows_live, cols_live, weight, bias, grad_out)
    taps = weight.shape[1]
    return pl.pallas_call(
        functools.partial(hand_over, own, taps),
        out_shape=(
            jax.ShapeDtypeStruct(grad_out.shape, BF16),
            jax.ShapeDtypeStruct((own, taps), F32),
            jax.ShapeDtypeStruct((own,), F32),
        ),
        in_specs=[vmem, vmem],
        out_specs=(hbm, vmem, pl.BlockSpec(memory_space=pltpu.SMEM)),
        scratch_shapes=[pltpu.SMEM((own, LANES), F32), dma((2,))],
        compiler_params=pltpu.CompilerParams(vmem_limit_bytes=4 * 1024 * 1024),
    )(landed, sums)


def solution(mesh):
    nx, ny = mesh.shape["gx"], mesh.shape["gy"]
    span = 4 if nx % 4 == 0 else 1
    in_specs = (P(None, "gx", "gy", None), P(), P(), P(), P(), P("gy", "gx", None, None))
    out_specs = (P("gy", "gx", None, None), P("gy", None), P("gy"))
    run = functools.partial(local, nx, ny, span)
    return jax.shard_map(run, mesh=mesh, in_specs=in_specs, out_specs=out_specs, check_vma=False)
```

time: 60.4 us -> 47.2 us (0.78)
  local copies, waits for them, and re-layouts: 6.79 us -> 0 us
  Pallas kernels: 52.7 us -> 46.5 us
    pallas_call x1 -> x2, Pallas kernels: 52.7 us -> 46.5 us  [the longest x1 45.1 us: local(): pl.pallas_call(functools.partial(kernel, dims), out_shape=(pltpu.VMEM(gra...]
    unnamed x13 -> x0, local copies, waits for them, and re-layouts: 5.53 us -> none
    slice x2 -> x0, local copies, waits for them, and re-layouts: 1.26 us -> none  [local(): return (stem, sums[:own, :taps], sums[:own, taps])]
where the time goes in v2:
time: 47.2 us; the launch traced here: 47.1 us
  Pallas kernels  46.5 us (99%)
  between operations  0.64 us (1%)
    pallas_call x1, Pallas kernels, local(): pl.pallas_call(functools.partial(kernel, dims), out_shape=(pltpu.VMEM(gra...  45.1 us
    pallas_call x1, Pallas kernels, local(): pl.pallas_call(functools.partial(hand_over, own, taps), out_shape=(jax.Sh...  1.38 us

profile of v2, /device:TPU:1, one launch (start us, length us, event | category | flops | bytes accessed | tf_op | source)
XLA Modules:
  0.0 47.1 jit_solution(14929108480980228770)
XLA Ops:
  0.6 45.1 %shard_map.85 = (bf16[2,4,256,128]{3,2,1,0:T(8,128)(2,1)S(1)}, f32[2,128]{1,0:T(2,128)S(1)}) custom-call(bf16[4,8,32,256]{3,2,1,0:T(8,128)(2,1)} %fields_hbm.1, s32[32]{0:T(128)} %rows_hbm.1, s32[16]{0:T(128)} %cols_hbm.1, bf16[32,108]{1,0:T(8,128)(2,1)} %weight_hbm.1, f32[32]{0:T(128)} %bias_hbm.1, bf16[2,4,256,128]{3,2,1,0:T(8,128)(2,1)} %grad_hbm.1), custom_call_target="tpu_custom_call" | custom-call | tf_op jit(solution)/shard_map/pallas_call | solution.py:398
  45.7 1.4 %shard_map.86 = (bf16[2,4,256,128]{3,2,1,0:T(8,128)(2,1)}, f32[2,108]{1,0:T(2,128)}, f32[2]{0:T(128)}) custom-call(bf16[2,4,256,128]{3,2,1,0:T(8,128)(2,1)S(1)} %get-tuple-element.5.landed, f32[2,128]{1,0:T(2,128)S(1)} %get-tuple-element.6.sums), custom_call_target="tpu_custom_call" | custom-call | tf_op jit(solution)/shard_map/pallas_call | solution.py:443

commit v3 on v2

--- a/solution.py
+++ b/solution.py
@@ -11,8 +11,8 @@
 F32 = jnp.float32
 BF16 = jnp.bfloat16
 LANES = 128
-EARLY = 0
-SOON = 1
+AFTER = 8
+CUTS = (2, 6, 10)
 FIRST = 6
 GROUP = 4
 
@@ -29,13 +29,14 @@
     rows32, lines, border, spread, taps_b, band, patches, acc, slope, stage, grads, grad_pre,
     part, part_in, xpart, xpart_in, zpart, zpart_in,
     load_sem, halo_send, halo_recv, grad_send, grad_recv, stem_send, stem_recv,
-    part_send, part_recv, x_send, x_recv, z_send, z_recv,
+    part_send, part_recv, x_send, x_recv, z_send, z_recv, seam_sem, told_sem,
 ):
     nx, ny, span, cin, cout, cap_x, cap_y, depth = dims
     half_x, half_y, half_z = cap_x // 2, cap_y // 2, depth // 2
     own = cout // ny
     planes = nx // span
     own = cout // ny
+    half = planes // 2
     cells = half_x * half_z
     tall = patches.shape[1]
     window = band.shape[1] // 9
@@ -44,16 +45,22 @@
     gx, gy = lax.axis_index("gx"), lax.axis_index("gy")
     iz, ix = gx // span, gx % span
 
+    at_seam = (iz == half - 1) | (iz == half)
+    across = jnp.where(iz == half, gx - span, gx + span)
+
     def wrap(value, size):
-        return lax.rem(value + size, size)
-
-    def farthest_first(step):
-        half = (step + 1) // 2
-        return ny // 2 + jnp.where(step % 2 == 1, half, -half)
+        return jnp.where(value >= size, value - size, value)
+
+    order = [ny // 2]
+    for step in range(1, ny // 2):
+        order += [ny // 2 + step, ny // 2 - step]
 
     def x_peer(d):
         return (iz * span + wrap(ix + d, span), gy)
 
+    def half_peer(d):
+        return ((iz // half * half + wrap(iz % half + d, half)) * span + ix, gy)
+
     def z_peer(d):
         return (wrap(iz + d, planes) * span + ix, gy)
 
@@ -62,9 +69,28 @@
     def greet(device):
         pl.semaphore_signal(barrier, inc=1, device_id=device, device_id_type=MESH)
 
-    def greet_y(step, carry):
-        greet((gx, wrap(gy + farthest_first(step), ny)))
-        return carry
+    for d in order:
+        greet((gx, wrap(gy + d, ny)))
+    above_us, below_us = gx > 0, gx < nx - 1
+
+    @pl.when(above_us)
+    def _():
+        greet((gx - 1, gy))
+        greet((gx - 1, wrap(gy + ny - 1, ny)))
+
+    @pl.when(below_us)
+    def _():
+        greet((gx + 1, gy))
+        greet((gx + 1, wrap(gy + 1, ny)))
+
+    for d in range(1, span):
+        greet(x_peer(d))
+    for d in range(1, half):
+        greet(half_peer(d))
+    if half:
+        @pl.when(at_seam)
+        def _():
+            greet((across, gy))
 
     load = pltpu.make_async_copy(fields_hbm, fields, load_sem.at[0])
     load.start()
@@ -82,19 +108,16 @@
     ]
     for copy in small:
         copy.start()
-    lax.fori_loop(0, ny - 1, greet_y, 0)
-    for dx, dy in ((1, 0), (-1, 0), (1, 1), (-1, -1)):
-        greet((wrap(gx + dx, nx), wrap(gy + dy, ny)))
-    for d in range(1, span):
-        greet(x_peer(d))
-    for d in range(1, planes):
-        greet(z_peer(d))
-    pl.semaphore_wait(barrier, ny - 1 + 4 + span - 1 + planes - 1)
+    guests = ny - 1 + span - 1
+    guests = guests + jnp.where(above_us, 2, 0) + jnp.where(below_us, 2, 0)
+    if half:
+        guests = guests + half - 1 + jnp.where(at_seam, 1, 0)
+    pl.semaphore_wait(barrier, guests)
 
     def halo_copy(index, src, dst, dx, dy):
         return pltpu.make_async_remote_copy(
             src_ref=src, dst_ref=dst, send_sem=halo_send.at[index], recv_sem=halo_recv.at[index],
-            device_id=(wrap(gx + dx, nx), wrap(gy + dy, ny)), device_id_type=MESH,
+            device_id=(gx + dx, wrap(gy + dy, ny)), device_id_type=MESH,
         )
 
     def grad_copy(d):
@@ -106,13 +129,14 @@
             device_id=(gx, to), device_id_type=MESH,
         )
 
-    def start_grad(step, carry):
-        grad_copy(farthest_first(step)).start()
-        return carry
-
     rows_out = halo_copy(0, fields_hbm.at[:, cap_x - 1], above, 1, 0)
-    rows_out.start()
-    lax.fori_loop(0, min(FIRST, ny - 1), start_grad, 0)
+
+    @pl.when(below_us)
+    def _():
+        rows_out.start()
+
+    for d in order[:FIRST]:
+        grad_copy(d).start()
 
     load.wait()
     for x in range(cap_x):
@@ -129,8 +153,18 @@
     side_out = halo_copy(1, side, side_in, 0, 1)
     side_out.start()
     corner_out = halo_copy(2, side, corner_in, 1, 1)
-    corner_out.start()
-    lax.fori_loop(min(FIRST, ny - 1), ny - 1, start_grad, 0)
+
+    @pl.when(below_us)
+    def _():
+        corner_out.start()
+
+    for d in order[FIRST:]:
+        grad_copy(d).start()
+
+    if half:
+        @pl.when(at_seam)
+        def _():
+            pl.semaphore_signal(seam_sem, inc=1, device_id=(across, gy), device_id_type=MESH)
 
     z_at = lax.broadcasted_iota(jnp.int32, (depth, 3 * half_z), 0)
     n_at = lax.broadcasted_iota(jnp.int32, (depth, 3 * half_z), 1)
@@ -158,9 +192,13 @@
             value = jnp.where(ext_y == 2 * i + b, by_tap[b], value)
         band[i * cout:(i + 1) * cout, :] = value.astype(BF16)
 
-    rows_out.wait_recv()
     side_out.wait_recv()
-    corner_out.wait_recv()
+
+    @pl.when(above_us)
+    def _():
+        rows_out.wait_recv()
+        corner_out.wait_recv()
+
     edge_x = cap_x - rows_ref[gx]
     edge_y = cap_y - cols_ref[gy]
     inner_x = gx > 0
@@ -236,20 +274,11 @@
             stage[o, p] = (pre * sigma).astype(BF16)
             slope[p, rows, :] = jnp.where(live, sigma * (1.0 + pre * (1.0 - sigma)), 0.0)
 
-    def forward(step, carry):
-        d = farthest_first(step)
-        for part_of in range(own):
-            activate(wrap(gy + d, ny) * own + part_of)
+    def forward(o, carry):
+        activate(o)
         return carry
 
-    def start_stem(step, carry):
-        stem_copy(farthest_first(step)).start()
-        return carry
-
-    lax.fori_loop(0, ny - 1, forward, 0)
-    for part_of in range(own):
-        activate(gy * own + part_of)
-    lax.fori_loop(0, min(EARLY, ny - 1), start_stem, 0)
+    lax.fori_loop(0, cout, forward, 0)
     keep = pltpu.make_async_copy(
         stage.at[pl.ds(gy * own, own)],
         stem_hbm.at[:, :, pl.ds(gy * half_y, half_y), :],
@@ -257,14 +286,23 @@
     )
     keep.start()
 
+    if half:
+        @pl.when(at_seam)
+        def _():
+            pl.semaphore_wait(seam_sem, 1)
+            for d in range(1, half):
+                pl.semaphore_signal(
+                    told_sem, inc=1, device_id=half_peer(d), device_id_type=MESH
+                )
+
     mine.wait()
 
-    def wait_grad(d, carry):
+    for d in order[:AFTER]:
         grad_copy(d).wait_recv()
-        return carry
-
-    lax.fori_loop(1, ny, wait_grad, 0)
-    lax.fori_loop(min(EARLY, ny - 1), min(SOON, ny - 1), start_stem, 0)
+    for d in order[:CUTS[0]]:
+        stem_copy(d).start()
+    for d in order[AFTER:]:
+        grad_copy(d).wait_recv()
 
     def chain(o, carry):
         rows = pl.ds(pl.multiple_of(o * half_y, half_y), half_y)
@@ -312,18 +350,15 @@
             device_id=(gx, to), device_id_type=MESH,
         )
 
-    def start_part(step, carry):
-        part_copy(farthest_first(step)).start()
-        return carry
-
-    lax.fori_loop(0, ny - 1, start_part, 0)
-    lax.fori_loop(min(SOON, ny - 1), ny - 1, start_stem, 0)
-
-    def take_part(d, held):
+    for d in order:
+        part_copy(d).start()
+    for d in order[CUTS[0]:CUTS[1]]:
+        stem_copy(d).start()
+    held = part[gy]
+    for d in order:
         part_copy(d).wait_recv()
-        return held + part_in[d]
-
-    xpart[...] = lax.fori_loop(1, ny, take_part, part[gy])
+        held = held + part_in[d]
+    xpart[...] = held
 
     def x_copy(d):
         return pltpu.make_async_remote_copy(
@@ -341,32 +376,42 @@
 
     for d in range(1, span):
         x_copy(d).start()
+    for d in order[CUTS[1]:CUTS[2]]:
+        stem_copy(d).start()
     xpart_in[ix] = xpart[...]
     for d in range(1, span):
         x_copy(d).wait_recv()
     zpart[...] = sum([xpart_in[i] for i in range(1, span)], xpart_in[0])
+    if half:
+        @pl.when(jnp.logical_not(at_seam))
+        def _():
+            pl.semaphore_wait(told_sem, 1)
+
     for d in range(1, planes):
         z_copy(d).start()
+    for d in order[CUTS[2]:]:
+        stem_copy(d).start()
     zpart_in[iz] = zpart[...]
     for d in range(1, planes):
         z_copy(d).wait_recv()
     sums_ref[...] = sum([zpart_in[i] for i in range(1, planes)], zpart_in[0])
 
-    def finish(d, carry):
+    for d in order:
         stem_copy(d).wait_recv()
         stem_copy(d).wait_send()
         grad_copy(d).wait_send()
         part_copy(d).wait_send()
-        return carry
-
-    lax.fori_loop(1, ny, finish, 0)
     for d in range(1, span):
         x_copy(d).wait_send()
     for d in range(1, planes):
         z_copy(d).wait_send()
-    rows_out.wait_send()
     side_out.wait_send()
-    corner_out.wait_send()
+
+    @pl.when(below_us)
+    def _():
+        rows_out.wait_send()
+        corner_out.wait_send()
+
     keep.wait()
 
 
@@ -434,6 +479,7 @@
             dma((7,)), dma((3,)), dma((3,)),
             dma((ny,)), dma((ny,)), dma((ny,)), dma((ny,)), dma((ny,)), dma((ny,)),
             dma((span,)), dma((span,)), dma((planes,)), dma((planes,)),
+            pltpu.SemaphoreType.REGULAR, pltpu.SemaphoreType.REGULAR,
         ],
         compiler_params=pltpu.CompilerParams(
             collective_id=0, has_side_effects=True, vmem_limit_bytes=63 * 1024 * 1024

time: 47.2 us -> 45.3 us (0.960)
  Pallas kernels: 46.5 us -> 44.5 us
    pallas_call x1, Pallas kernels: 45.1 us -> 43.2 us  [local(): pl.pallas_call(functools.partial(kernel, dims), out_shape=(pltpu.VMEM(gra...]
where the time goes in v3:
time: 45.3 us; the launch traced here: 45.2 us
  Pallas kernels  44.5 us (98%)
  between operations  0.64 us (1%)
    pallas_call x1, Pallas kernels, local(): pl.pallas_call(functools.partial(kernel, dims), out_shape=(pltpu.VMEM(gra...  43.2 us
    pallas_call x1, Pallas kernels, local(): pl.pallas_call(functools.partial(hand_over, own, taps), out_shape=(jax.Sh...  1.38 us

profile of v3, /device:TPU:1, one launch (start us, length us, event | category | flops | bytes accessed | tf_op | source)
XLA Modules:
  0.0 45.2 jit_solution(18410063879725613772)
XLA Ops:
  0.6 43.2 %shard_map.85 = (bf16[2,4,256,128]{3,2,1,0:T(8,128)(2,1)S(1)}, f32[2,128]{1,0:T(2,128)S(1)}) custom-call(bf16[4,8,32,256]{3,2,1,0:T(8,128)(2,1)} %fields_hbm.1, s32[32]{0:T(128)} %rows_hbm.1, s32[16]{0:T(128)} %cols_hbm.1, bf16[32,108]{1,0:T(8,128)(2,1)} %weight_hbm.1, f32[32]{0:T(128)} %bias_hbm.1, bf16[2,4,256,128]{3,2,1,0:T(8,128)(2,1)} %grad_hbm.1), custom_call_target="tpu_custom_call" | custom-call | tf_op jit(solution)/shard_map/pallas_call | solution.py:443
  43.8 1.4 %shard_map.86 = (bf16[2,4,256,128]{3,2,1,0:T(8,128)(2,1)}, f32[2,108]{1,0:T(2,128)}, f32[2]{0:T(128)}) custom-call(bf16[2,4,256,128]{3,2,1,0:T(8,128)(2,1)S(1)} %get-tuple-element.5.landed, f32[2,128]{1,0:T(2,128)S(1)} %get-tuple-element.6.sums), custom_call_target="tpu_custom_call" | custom-call | tf_op jit(solution)/shard_map/pallas_call | solution.py:489

commit v4 on v3

--- a/solution.py
+++ b/solution.py
@@ -11,8 +11,7 @@
 F32 = jnp.float32
 BF16 = jnp.bfloat16
 LANES = 128
-AFTER = 8
-CUTS = (2, 6, 10)
+CUTS = (1, 3, 7)
 FIRST = 6
 GROUP = 4
 
@@ -295,69 +294,74 @@
                     told_sem, inc=1, device_id=half_peer(d), device_id_type=MESH
                 )
 
-    mine.wait()
-
-    for d in order[:AFTER]:
+    sources = [wrap(gy + ny - d, ny) for d in order] + [gy]
+    per = cout // 2
+
+    def part_copy(slot):
+        return pltpu.make_async_remote_copy(
+            src_ref=part.at[slot], dst_ref=part_in.at[slot],
+            send_sem=part_send.at[slot], recv_sem=part_recv.at[slot],
+            device_id=(gx, sources[slot]), device_id_type=MESH,
+        )
+
+    def backward(group):
+        slots = range(group * ny // 2, (group + 1) * ny // 2)
+        for slot in slots:
+            for i in range(own):
+                o = sources[slot] * own + i
+                rows = pl.ds(pl.multiple_of(o * half_y, half_y), half_y)
+                at = (slot * own + i) * half_y
+                for p in range(half_x):
+                    value = (grads[o, p].astype(F32) * slope[p, rows, :]).astype(BF16)
+                    grad_pre[p, at:at + half_y, :] = value.astype(F32)
+        first = slots[0] * own * half_y
+        corr = jnp.zeros((GROUP * per, 9 * window), F32)
+        bias_sum = jnp.zeros((per, cells), F32)
+        for m in range(reach):
+            values = [
+                jnp.concatenate(
+                    [
+                        grad_pre[p, pl.ds(first + m * GROUP + i, per, stride=half_y), :]
+                        for p in range(half_x)
+                    ],
+                    axis=1,
+                )
+                for i in range(GROUP)
+            ]
+            bias_sum = bias_sum + sum(values[1:], values[0])
+            corr = corr + nt_dot(jnp.concatenate(values, axis=0).astype(BF16), windows(m))
+        total = jnp.zeros((per, LANES), F32)
+        for b in range(3):
+            picked = jnp.zeros((per, 9 * window), F32)
+            for i in range(GROUP):
+                picked = jnp.where(ext_y == 2 * i + b, corr[i * per:(i + 1) * per, :], picked)
+            high = picked.astype(BF16)
+            low = (picked - high.astype(F32)).astype(BF16)
+            total = total + (nt_dot(high, taps_b[b]) + nt_dot(low, taps_b[b]))
+        lane = lax.broadcasted_iota(jnp.int32, (per, LANES), 1)
+        total = jnp.where(lane == cin * 27, jnp.sum(bias_sum, axis=1, keepdims=True), total)
+        for slot in slots:
+            at = (slot - slots[0]) * own
+            part[slot] = total[at:at + own]
+        for slot in slots:
+            if slot < ny - 1:
+                part_copy(slot).start()
+
+    for d in order[:ny // 2]:
         grad_copy(d).wait_recv()
     for d in order[:CUTS[0]]:
         stem_copy(d).start()
-    for d in order[AFTER:]:
+    backward(0)
+    mine.wait()
+    for d in order[ny // 2:]:
         grad_copy(d).wait_recv()
-
-    def chain(o, carry):
-        rows = pl.ds(pl.multiple_of(o * half_y, half_y), half_y)
-        for p in range(half_x):
-            value = (grads[o, p].astype(F32) * slope[p, rows, :]).astype(BF16)
-            grad_pre[p, rows, :] = value.astype(F32)
-        return carry
-
-    lax.fori_loop(0, cout, chain, 0)
-
-    corr = jnp.zeros((GROUP * cout, 9 * window), F32)
-    bias_sum = jnp.zeros((cout, cells), F32)
-    for m in range(reach):
-        values = [
-            jnp.concatenate(
-                [
-                    grad_pre[p, pl.ds(m * GROUP + i, cout, stride=half_y), :]
-                    for p in range(half_x)
-                ],
-                axis=1,
-            )
-            for i in range(GROUP)
-        ]
-        bias_sum = bias_sum + sum(values[1:], values[0])
-        corr = corr + nt_dot(jnp.concatenate(values, axis=0).astype(BF16), windows(m))
-    total = jnp.zeros((cout, LANES), F32)
-    for b in range(3):
-        picked = jnp.zeros((cout, 9 * window), F32)
-        for i in range(GROUP):
-            picked = jnp.where(ext_y == 2 * i + b, corr[i * cout:(i + 1) * cout, :], picked)
-        high = picked.astype(BF16)
-        low = (picked - high.astype(F32)).astype(BF16)
-        total = total + (nt_dot(high, taps_b[b]) + nt_dot(low, taps_b[b]))
-    lane = lax.broadcasted_iota(jnp.int32, (cout, LANES), 1)
-    total = jnp.where(lane == cin * 27, jnp.sum(bias_sum, axis=1, keepdims=True), total)
-
-    for j in range(ny):
-        part[j] = total[j * own:(j + 1) * own, :]
-
-    def part_copy(d):
-        to = wrap(gy + d, ny)
-        return pltpu.make_async_remote_copy(
-            src_ref=part.at[to], dst_ref=part_in.at[d],
-            send_sem=part_send.at[d], recv_sem=part_recv.at[d],
-            device_id=(gx, to), device_id_type=MESH,
-        )
-
-    for d in order:
-        part_copy(d).start()
+    backward(1)
     for d in order[CUTS[0]:CUTS[1]]:
         stem_copy(d).start()
-    held = part[gy]
-    for d in order:
-        part_copy(d).wait_recv()
-        held = held + part_in[d]
+    held = part[ny - 1]
+    for slot in range(ny - 1):
+        part_copy(slot).wait_recv()
+        held = held + part_in[slot]
     xpart[...] = held
 
     def x_copy(d):
@@ -400,7 +404,8 @@
         stem_copy(d).wait_recv()
         stem_copy(d).wait_send()
         grad_copy(d).wait_send()
-        part_copy(d).wait_send()
+    for slot in range(ny - 1):
+        part_copy(slot).wait_send()
     for d in range(1, span):
         x_copy(d).wait_send()
     for d in range(1, planes):

time: 45.3 us -> 43.6 us (0.962)
  Pallas kernels: 44.5 us -> 42.8 us
    pallas_call x1, Pallas kernels: 43.2 us -> 41.4 us  [local(): pl.pallas_call(functools.partial(kernel, dims), out_shape=(pltpu.VMEM(gra...]
where the time goes in v4:
time: 43.6 us; the launch traced here: 43.4 us
  Pallas kernels  42.8 us (98%)
  between operations  0.64 us (1%)
    pallas_call x1, Pallas kernels, local(): pl.pallas_call(functools.partial(kernel, dims), out_shape=(pltpu.VMEM(gra...  41.4 us
    pallas_call x1, Pallas kernels, local(): pl.pallas_call(functools.partial(hand_over, own, taps), out_shape=(jax.Sh...  1.38 us

profile of v4, /device:TPU:1, one launch (start us, length us, event | category | flops | bytes accessed | tf_op | source)
XLA Modules:
  0.0 43.4 jit_solution(14220859371720065584)
XLA Ops:
  0.6 41.4 %shard_map.85 = (bf16[2,4,256,128]{3,2,1,0:T(8,128)(2,1)S(1)}, f32[2,128]{1,0:T(2,128)S(1)}) custom-call(bf16[4,8,32,256]{3,2,1,0:T(8,128)(2,1)} %fields_hbm.1, s32[32]{0:T(128)} %rows_hbm.1, s32[16]{0:T(128)} %cols_hbm.1, bf16[32,108]{1,0:T(8,128)(2,1)} %weight_hbm.1, f32[32]{0:T(128)} %bias_hbm.1, bf16[2,4,256,128]{3,2,1,0:T(8,128)(2,1)} %grad_hbm.1), custom_call_target="tpu_custom_call" | custom-call | tf_op jit(solution)/shard_map/pallas_call | solution.py:448
  42.0 1.4 %shard_map.86 = (bf16[2,4,256,128]{3,2,1,0:T(8,128)(2,1)}, f32[2,108]{1,0:T(2,128)}, f32[2]{0:T(128)}) custom-call(bf16[2,4,256,128]{3,2,1,0:T(8,128)(2,1)S(1)} %get-tuple-element.5.landed, f32[2,128]{1,0:T(2,128)S(1)} %get-tuple-element.6.sums), custom_call_target="tpu_custom_call" | custom-call | tf_op jit(solution)/shard_map/pallas_call | solution.py:494

commit v5 on v4

--- a/solution.py
+++ b/solution.py
@@ -11,8 +11,8 @@
 F32 = jnp.float32
 BF16 = jnp.bfloat16
 LANES = 128
-CUTS = (1, 3, 7)
-FIRST = 6
+CUTS = (1, 3, 8)
+FIRST = 2
 GROUP = 4
 
 

time: 43.6 us -> 43.6 us (level)
  no operation moved by 1% of the time
where the time goes in v5:
time: 43.6 us; the launch traced here: 43.4 us
  Pallas kernels  42.8 us (98%)
  between operations  0.64 us (1%)
    pallas_call x1, Pallas kernels, local(): pl.pallas_call(functools.partial(kernel, dims), out_shape=(pltpu.VMEM(gra...  41.4 us
    pallas_call x1, Pallas kernels, local(): pl.pallas_call(functools.partial(hand_over, own, taps), out_shape=(jax.Sh...  1.38 us

profile of v5, /device:TPU:1, one launch (start us, length us, event | category | flops | bytes accessed | tf_op | source)
XLA Modules:
  0.0 43.4 jit_solution(5053793390843391363)
XLA Ops:
  0.6 41.4 %shard_map.85 = (bf16[2,4,256,128]{3,2,1,0:T(8,128)(2,1)S(1)}, f32[2,128]{1,0:T(2,128)S(1)}) custom-call(bf16[4,8,32,256]{3,2,1,0:T(8,128)(2,1)} %fields_hbm.1, s32[32]{0:T(128)} %rows_hbm.1, s32[16]{0:T(128)} %cols_hbm.1, bf16[32,108]{1,0:T(8,128)(2,1)} %weight_hbm.1, f32[32]{0:T(128)} %bias_hbm.1, bf16[2,4,256,128]{3,2,1,0:T(8,128)(2,1)} %grad_hbm.1), custom_call_target="tpu_custom_call" | custom-call | tf_op jit(solution)/shard_map/pallas_call | solution.py:448
  42.0 1.4 %shard_map.86 = (bf16[2,4,256,128]{3,2,1,0:T(8,128)(2,1)}, f32[2,108]{1,0:T(2,128)}, f32[2]{0:T(128)}) custom-call(bf16[2,4,256,128]{3,2,1,0:T(8,128)(2,1)S(1)} %get-tuple-element.5.landed, f32[2,128]{1,0:T(2,128)S(1)} %get-tuple-element.6.sums), custom_call_target="tpu_custom_call" | custom-call | tf_op jit(solution)/shard_map/pallas_call | solution.py:494
